TPU v7x, 32 devices: a whole 2x2x4 slice. The times are simulated.
32 devices in a mesh: lat: 4 (over y, x), lon: 8 (over z, core).
Axes of the slice: x: 2, y: 2, z: 4, core: 2. Of those that a mesh axis runs over, the one named last changes fastest.
Arguments:
- field: bfloat16 [8, 48, 192, 192], P(None, 'lat', 'lon'), may hold values from -6 to 6
- a_norm_one: float32 [192], replicated, may hold values from 0.1 to 1.9
- a_project: bfloat16 [192, 576], replicated, may hold values from -0.4375 to 0.4375
- a_bias: float32 [6, 144, 144], replicated, may hold values from -4 to 240
- a_output: bfloat16 [192, 192], replicated, may hold values from -0.4375 to 0.4375
- a_norm_two: float32 [192], replicated, may hold values from 0.1 to 1.9
- a_raise: bfloat16 [192, 768], replicated, may hold values from -0.4375 to 0.4375
- a_lower: bfloat16 [768, 192], replicated, may hold values from -0.21875 to 0.21875
- merge_norm_gain: float32 [768], replicated, may hold values from 0.1 to 1.9
- merge_weight: bfloat16 [768, 384], replicated, may hold values from -0.21875 to 0.21875
- b_norm_one: float32 [384], replicated, may hold values from 0.1 to 1.9
- b_project: bfloat16 [384, 1152], replicated, may hold values from -0.3125 to 0.3125
- b_bias: float32 [12, 144, 144], replicated, may hold values from -4 to 240
- b_output: bfloat16 [384, 384], replicated, may hold values from -0.3125 to 0.3125
- b_norm_two: float32 [384], replicated, may hold values from 0.1 to 1.9
- b_raise: bfloat16 [384, 1536], replicated, may hold values from -0.3125 to 0.3125
- b_lower: bfloat16 [1536, 384], replicated, may hold values from -0.15625 to 0.15625
- up_first: bfloat16 [384, 768], replicated, may hold values from -0.3125 to 0.3125
- up_norm: float32 [192], replicated, may hold values from 0.1 to 1.9
- up_second: bfloat16 [192, 192], replicated, may hold values from -0.4375 to 0.4375
Outputs:
- fine: bfloat16 [8, 48, 192, 192], P(None, 'lat', 'lon')
All inputs are finite; a program needn't handle non-finite values.
Results may differ from a plain program's by a relative error of at most 0.023.
Values may be sent and summed in bfloat16 or wider, within the bound.
A program may use at most 192 MiB of HBM per device.

v0:
```python
import functools
import math

import jax
import jax.numpy as jnp
import numpy as np
from jax import lax
from jax.experimental import pallas as pl
from jax.experimental.pallas import tpu as pltpu
from jax.sharding import PartitionSpec as P

WIN_P = 2
WIN_LAT = 6
WIN_LON = 12
HALF_LAT = WIN_LAT // 2
HALF_LON = WIN_LON // 2
HEAD = 32
LANES = 128
EPS = 1e-05
EXCLUDED = -1e30
MESH = pl.DeviceIdType.MESH
BF16 = jnp.bfloat16
F32 = jnp.float32


def pad16(count):
    return -(-count // 16) * 16


class Grid:
    def __init__(self, rows, columns):
        self.rows, self.columns = rows, columns
        self.local = WIN_P * rows * columns
        self.windows = self.local // (WIN_P * WIN_LAT * WIN_LON)
        counts = [
            WIN_P * HALF_LAT * (columns - HALF_LON),
            WIN_P * (rows - HALF_LAT) * HALF_LON,
            WIN_P * HALF_LAT * HALF_LON,
        ]
        self.sizes = [pad16(count) for count in counts]
        self.starts = [0, self.sizes[0], self.sizes[0] + self.sizes[1]]
        self.halo = sum(self.sizes)

    def natural(self, level, row, column):
        return (level * self.rows + row) * self.columns + column

    def slot(self, level, row, column):
        wide = self.columns - HALF_LON
        tall = self.rows - HALF_LAT
        if row < HALF_LAT and column >= HALF_LON:
            return (level * HALF_LAT + row) * wide + column - HALF_LON
        if row >= HALF_LAT and column < HALF_LON:
            return self.starts[1] + (level * tall + row - HALF_LAT) * HALF_LON + column
        return self.starts[2] + (level * HALF_LAT + row) * HALF_LON + column

    def send(self):
        matrix = np.zeros((self.halo, self.local), np.float32)
        for level in range(WIN_P):
            for row in range(self.rows):
                for column in range(self.columns):
                    if row < HALF_LAT or column < HALF_LON:
                        matrix[self.slot(level, row, column), self.natural(level, row, column)] = 1
        return matrix

    def gather(self):
        own = np.zeros((self.local, self.local), np.float32)
        halo = np.zeros((self.local, self.halo), np.float32)
        index = 0
        for top in range(0, self.rows, WIN_LAT):
            for left in range(0, self.columns, WIN_LON):
                for level in range(WIN_P):
                    for row in range(top + HALF_LAT, top + HALF_LAT + WIN_LAT):
                        for column in range(left + HALF_LON, left + HALF_LON + WIN_LON):
                            if row < self.rows and column < self.columns:
                                own[index, self.natural(level, row, column)] = 1
                            else:
                                halo[index, self.slot_ahead(level, row, column)] = 1
                            index += 1
        return own, halo

    def slot_ahead(self, level, row, column):
        return self.slot(
            level,
            row - self.rows if row >= self.rows else row,
            column - self.columns if column >= self.columns else column,
        )

    def quarters(self):
        matrix = np.zeros((self.local, self.local), np.float32)
        index = 0
        for r in range(2):
            for t in range(2):
                for level in range(WIN_P):
                    for row in range(r, self.rows, 2):
                        for column in range(t, self.columns, 2):
                            matrix[index, self.natural(level, row, column)] = 1
                            index += 1
        return matrix


def dot(a, b):
    return jnp.dot(a, b, preferred_element_type=F32)


def pick(matrix, values):
    return dot(matrix, values).astype(BF16)


def layer_norm(values, gain):
    average = jnp.mean(values, axis=-1, keepdims=True)
    centred = values - average
    variance = jnp.mean(centred * centred, axis=-1, keepdims=True)
    return centred * lax.rsqrt(variance + EPS) * gain


def gelu(x):
    return 0.5 * x * (1.0 + lax.erf(x * math.sqrt(0.5)))


def attend(q_ref, k_ref, v_ref, out_ref, rows, bias_ref, mask):
    size = mask.shape[0]
    width = q_ref.shape[-1]
    for start in range(0, width, LANES):
        lanes = slice(start, min(start + LANES, width))
        span = lanes.stop - start
        heads = span // HEAD
        first = start // HEAD
        q = q_ref[rows, lanes]
        lane = lax.broadcasted_iota(jnp.int32, (size, span), 1) // HEAD
        stack = jnp.concatenate(
            [jnp.where(lane == head, q, jnp.zeros_like(q)) for head in range(heads)], axis=0
        )
        scores = lax.dot_general(
            stack, k_ref[rows, lanes], (((1,), (1,)), ((), ())), preferred_element_type=F32
        )
        scores = scores * (1.0 / math.sqrt(HEAD)) + bias_ref[first * size : (first + heads) * size, :]
        scores = (scores.reshape(heads, size, size) + mask[None]).reshape(heads * size, size)
        highest = jnp.max(scores, axis=-1, keepdims=True)
        raised = jnp.exp(scores - highest)
        total = jnp.sum(raised, axis=-1, keepdims=True)
        mixed = dot(raised.astype(BF16), v_ref[rows, lanes]) / total
        result = jnp.zeros((size, span), F32)
        for head in range(heads):
            result = jnp.where(lane == head, mixed[head * size : (head + 1) * size], result)
        out_ref[rows, lanes] = result.astype(BF16)


def feed_forward(after, gain, up_ref, down_ref):
    normed = layer_norm(after, gain).astype(BF16)
    total = after
    width = up_ref.shape[1]
    for start in range(0, width, 256):
        columns = slice(start, start + 256)
        hidden = gelu(dot(normed, up_ref[:, columns])).astype(BF16)
        total = total + dot(hidden, down_ref[columns, :])
    return total.astype(BF16)


def section(fine, coarse, lats, lons, *refs):
    (
        field, a_norm_one, a_project, a_bias, a_output, a_norm_two, a_raise, a_lower,
        merge_gain, merge_weight,
        b_norm_one, b_project, b_bias, b_output, b_norm_two, b_raise, b_lower,
        up_first, up_norm, up_second,
        fine_send, fine_own, fine_halo, fine_send_back, fine_own_back, fine_halo_back, quarter, quarter_back,
        coarse_send, coarse_own, coarse_halo, coarse_send_back, coarse_own_back, coarse_halo_back,
        level_mask, lat_mask,
        out,
        fine_normed, skip, coarse_in, coarse_normed, q_ref, k_ref, v_ref, attended, coarse_attended,
        qc_ref, kc_ref, vc_ref, parts,
        out_one, in_one, out_two, in_two, out_three, in_three, out_four, in_four,
        send_sems, recv_sems,
    ) = refs
    depth = field.shape[0]
    pairs = depth // WIN_P
    width = field.shape[2]
    size = WIN_P * WIN_LAT * WIN_LON
    level_size = field.shape[1]
    lat, lon = lax.axis_index("lat"), lax.axis_index("lon")
    lat_next, lat_last = lax.rem(lat + 1, lats), lax.rem(lat + lats - 1, lats)
    lon_next, lon_last = lax.rem(lon + 1, lons), lax.rem(lon + lons - 1, lons)
    behind = ((lat_last, lon), (lat, lon_last), (lat_last, lon_last))
    ahead = ((lat_next, lon), (lat, lon_next), (lat_next, lon_next))

    barrier = pltpu.get_barrier_semaphore()
    for device in behind + ahead:
        pl.semaphore_signal(barrier, inc=1, device_id=device, device_id_type=MESH)
    pl.semaphore_wait(barrier, 6)

    def copies(phase, pair, grid, source, target, devices):
        made = []
        for part in range(3):
            rows = pl.ds(grid.starts[part], grid.sizes[part])
            made.append(
                pltpu.make_async_remote_copy(
                    src_ref=source.at[pair, rows],
                    dst_ref=target.at[pair, rows],
                    send_sem=send_sems.at[phase, pair, part],
                    recv_sem=recv_sems.at[phase, pair, part],
                    device_id=devices[part],
                    device_id_type=MESH,
                )
            )
        return made

    phase_one = functools.partial(copies, 0, grid=fine, source=out_one, target=in_one, devices=behind)
    phase_two = functools.partial(copies, 1, grid=fine, source=out_two, target=in_two, devices=ahead)
    phase_three = functools.partial(copies, 2, grid=coarse, source=out_three, target=in_three, devices=behind)
    phase_four = functools.partial(copies, 3, grid=coarse, source=out_four, target=in_four, devices=ahead)

    def field_pair(pair):
        return jnp.concatenate([field[2 * pair + 1], field[lax.rem(2 * pair + 2, depth)]], axis=0)

    def level_flag(pair):
        return jnp.where(pair == pairs - 1, 1.0, 0.0).astype(F32)

    lat_flag = jnp.where(lat == lats - 1, 1.0, 0.0).astype(F32)

    def send_fine(pair, carry):
        normed = layer_norm(field_pair(pair).astype(F32), a_norm_one[...]).astype(BF16)
        fine_normed[pair] = normed
        out_one[pair] = pick(fine_send[...], normed)
        for copy in phase_one(pair):
            copy.start()
        return carry

    lax.fori_loop(0, pairs, send_fine, 0)

    project = a_project[...]
    for part in range(3):
        parts[part] = project[:, part * width : (part + 1) * width]

    def attend_fine(pair, carry):
        for copy in phase_one(pair):
            copy.wait_recv()
        tokens = (dot(fine_own[...], fine_normed[pair]) + dot(fine_halo[...], in_one[pair])).astype(BF16)
        for part, ref in enumerate((q_ref, k_ref, v_ref)):
            ref[...] = dot(tokens, parts[part]).astype(BF16)
        level = level_flag(pair) * level_mask[...]
        across = fine.columns // WIN_LON

        def window(index, inner):
            bottom = jnp.where(index >= fine.windows - across, lat_flag, 0.0)
            mask = level + bottom * lat_mask[...]
            rows = pl.ds(pl.multiple_of(index * size, size), size)
            attend(q_ref, k_ref, v_ref, attended.at[pair], rows, a_bias, mask)
            return inner

        lax.fori_loop(0, fine.windows, window, 0)
        out_two[pair] = pick(fine_send_back[...], attended[pair])
        for copy in phase_two(pair):
            copy.start()
        return carry

    lax.fori_loop(0, pairs, attend_fine, 0)

    def finish_fine(pair, carry):
        for copy in phase_two(pair):
            copy.wait_recv()
        mixed = (dot(fine_own_back[...], attended[pair]) + dot(fine_halo_back[...], in_two[pair])).astype(BF16)
        after = dot(quarter[...], field_pair(pair)) + dot(mixed, a_output[...])
        after = after.astype(BF16).astype(F32)
        state = feed_forward(after, a_norm_two[...], a_raise, a_lower)
        skip[pair] = state
        quarters = [state[i * size : (i + 1) * size].astype(F32) for i in range(4)]
        average = sum(jnp.sum(values, axis=-1, keepdims=True) for values in quarters) / (4 * width)
        centred = [values - average for values in quarters]
        variance = sum(jnp.sum(values * values, axis=-1, keepdims=True) for values in centred) / (4 * width)
        factor = lax.rsqrt(variance + EPS)
        merged = jnp.zeros((size, merge_weight.shape[1]), F32)
        for i in range(4):
            normed = (centred[i] * factor * merge_gain[i]).astype(BF16)
            merged = merged + dot(normed, merge_weight[i * width : (i + 1) * width, :])
        merged = merged.astype(BF16)
        coarse_in[pair] = merged
        normed = layer_norm(merged.astype(F32), b_norm_one[...]).astype(BF16)
        coarse_normed[pair] = normed
        out_three[pair] = pick(coarse_send[...], normed)
        for copy in phase_three(pair):
            copy.start()
        return carry

    lax.fori_loop(0, pairs, finish_fine, 0)

    def attend_coarse(pair, carry):
        for copy in phase_three(pair):
            copy.wait_recv()
        tokens = (dot(coarse_own[...], coarse_normed[pair]) + dot(coarse_halo[...], in_three[pair])).astype(BF16)
        double = tokens.shape[1]
        for part, ref in enumerate((qc_ref, kc_ref, vc_ref)):
            ref[...] = dot(tokens, b_project[:, part * double : (part + 1) * double]).astype(BF16)
        mask = level_flag(pair) * level_mask[...] + lat_flag * lat_mask[...]
        attend(qc_ref, kc_ref, vc_ref, coarse_attended.at[pair], pl.ds(0, size), b_bias, mask)
        out_four[pair] = pick(coarse_send_back[...], coarse_attended[pair])
        for copy in phase_four(pair):
            copy.start()
        return carry

    lax.fori_loop(0, pairs, attend_coarse, 0)

    def finish_coarse(pair, carry):
        for copy in phase_four(pair):
            copy.wait_recv()
        mixed = (
            dot(coarse_own_back[...], coarse_attended[pair]) + dot(coarse_halo_back[...], in_four[pair])
        ).astype(BF16)
        after = coarse_in[pair].astype(F32) + dot(mixed, b_output[...])
        after = after.astype(BF16).astype(F32)
        state = feed_forward(after, b_norm_two[...], b_raise, b_lower)
        raised = dot(state, up_first[...]).astype(BF16).astype(F32)
        raised = jnp.concatenate([raised[:, i * width : (i + 1) * width] for i in range(4)], axis=0)
        normed = layer_norm(raised, up_norm[...]).astype(BF16)
        total = (skip[pair].astype(F32) + dot(normed, up_second[...])).astype(BF16)
        total = pick(quarter_back[...], total)
        out[2 * pair + 1] = total[:level_size]
        out[lax.rem(2 * pair + 2, depth)] = total[level_size:]
        return carry

    lax.fori_loop(0, pairs, finish_coarse, 0)

    def drain(pair, carry):
        for phase in (phase_one, phase_two, phase_three, phase_four):
            for copy in phase(pair):
                copy.wait_send()
        return carry

    lax.fori_loop(0, pairs, drain, 0)


def body(
    lats, lons, field,
    a_norm_one, a_project, a_bias, a_output, a_norm_two, a_raise, a_lower,
    merge_norm_gain, merge_weight,
    b_norm_one, b_project, b_bias, b_output, b_norm_two, b_raise, b_lower,
    up_first, up_norm, up_second,
):
    depth, rows, columns, width = field.shape
    double = merge_weight.shape[1]
    pairs = depth // WIN_P
    size = WIN_P * WIN_LAT * WIN_LON
    fine, coarse = Grid(rows, columns), Grid(rows // 2, columns // 2)
    quarter = fine.quarters()

    def one_hot(matrix):
        return jnp.asarray(matrix.astype(BF16))

    fine_own, fine_halo = fine.gather()
    coarse_own, coarse_halo = coarse.gather()
    orders = [
        fine.send(), fine_own, fine_halo, fine_halo.T, quarter @ fine_own.T, quarter @ fine.send().T,
        quarter, quarter.T,
        coarse.send(), coarse_own, coarse_halo, coarse_halo.T, coarse_own.T, coarse.send().T,
    ]
    token = np.arange(size)
    level = token // (WIN_LAT * WIN_LON)
    edge = (token // WIN_LON) % WIN_LAT >= WIN_LAT - HALF_LAT
    masks = [
        np.where(kind[:, None] != kind[None, :], EXCLUDED, 0.0).astype(np.float32) for kind in (level, edge)
    ]
    operands = [
        field.reshape(depth, rows * columns, width),
        a_norm_one.reshape(1, -1), a_project, a_bias.reshape(-1, size), a_output, a_norm_two.reshape(1, -1),
        a_raise, a_lower,
        merge_norm_gain.reshape(4, 1, width), merge_weight,
        b_norm_one.reshape(1, -1), b_project, b_bias.reshape(-1, size), b_output, b_norm_two.reshape(1, -1),
        b_raise, b_lower,
        up_first, up_norm.reshape(1, -1), up_second,
    ]
    operands += [one_hot(matrix) for matrix in orders] + [jnp.asarray(mask) for mask in masks]
    vmem = pl.BlockSpec(memory_space=pltpu.VMEM)
    result = pl.pallas_call(
        functools.partial(section, fine, coarse, lats, lons),
        out_shape=jax.ShapeDtypeStruct((depth, rows * columns, width), BF16),
        in_specs=[vmem] * len(operands),
        out_specs=vmem,
        scratch_shapes=[
            pltpu.VMEM((pairs, fine.local, width), BF16),
            pltpu.VMEM((pairs, fine.local, width), BF16),
            pltpu.VMEM((pairs, coarse.local, double), BF16),
            pltpu.VMEM((pairs, coarse.local, double), BF16),
            pltpu.VMEM((fine.local, width), BF16),
            pltpu.VMEM((fine.local, width), BF16),
            pltpu.VMEM((fine.local, width), BF16),
            pltpu.VMEM((pairs, fine.local, width), BF16),
            pltpu.VMEM((pairs, coarse.local, double), BF16),
            pltpu.VMEM((coarse.local, double), BF16),
            pltpu.VMEM((coarse.local, double), BF16),
            pltpu.VMEM((coarse.local, double), BF16),
            pltpu.VMEM((3, width, width), BF16),
        ]
        + [pltpu.VMEM((pairs, fine.halo, width), BF16)] * 4
        + [pltpu.VMEM((pairs, coarse.halo, double), BF16)] * 4
        + [pltpu.SemaphoreType.DMA((4, pairs, 3)), pltpu.SemaphoreType.DMA((4, pairs, 3))],
        compiler_params=pltpu.CompilerParams(
            collective_id=0, has_side_effects=True, vmem_limit_bytes=56 * 1024 * 1024
        ),
    )(*operands)
    return result.reshape(field.shape)


def solution(mesh):
    in_specs = (P(None, "lat", "lon", None),) + (P(),) * 19
    return jax.shard_map(
        functools.partial(body, mesh.shape["lat"], mesh.shape["lon"]),
        mesh=mesh,
        in_specs=in_specs,
        out_specs=P(None, "lat", "lon", None),
        check_vma=False,
    )
```

profile of v0, /device:TPU:0, one launch (start us, length us, event | category | flops | bytes accessed | tf_op | source)
XLA Modules:
  0.0 76.0 jit_solution(1023186050764598725)
XLA Ops:
  0.0 1.2 %reshape.35.refs_10_ = f32[1,384]{1,0:T(1,128)} reshape(f32[384]{0:T(512)} %param.46) | data formatting | bytes 3072 | tf_op jit(solution)/shard_map/reshape | solution.py:365
  1.2 1.2 %reshape.37.refs_14_ = f32[1,384]{1,0:T(1,128)} reshape(f32[384]{0:T(512)} %param.50) | data formatting | bytes 3072 | tf_op jit(solution)/shard_map/reshape | solution.py:365
  2.5 1.4 %reshape.34.refs_8_ = f32[4,1,192]{2,1,0:T(1,128)} reshape(f32[768]{0:T(1024)} %param.44) | data formatting | bytes 6144 | tf_op jit(solution)/shard_map/reshape | solution.py:364
  3.8 1.9 %copy.37.refs_7_ = bf16[768,192]{1,0:T(8,128)(2,1)} copy(bf16[768,192]{0,1:T(8,128)(2,1)} %param.43) | data formatting | bytes 589824 | tf_op args[7]
  5.7 68.0 %shard_map.334 = bf16[8,288,192]{2,1,0:T(8,128)(2,1)} custom-call(bf16[8,288,192]{2,1,0:T(8,128)(2,1)} %bitcast.9, f32[1,192]{1,0:T(1,128)} %bitcast.11, bf16[192,576]{1,0:T(8,128)(2,1)} %refs_2_.1, f32[864,144]{1,0:T(8,128)} %bitcast.10, bf16[192,192]{1,0:T(8,128)(2,1)} %refs_4_.1, f32[1,192]{1,0:T(1,128)} %bitcast.12, bf16[192,768]{1,0:T(8,128)(2,1)} %refs_6_.1, ...), custom_call_target="tpu_custom_call" | custom-call | tf_op jit(solution)/shard_map/pallas_call | solution.py:371
  73.7 2.4 %copy.39 = bf16[8,12,24,192]{3,2,1,0:T(8,128)(2,1)} copy(bf16[8,12,24,192]{3,2,1,0:T(8,128)(2,1)} %bitcast.7) | data formatting | bytes 1769472
where the time goes:
time: 76.3 us; the launch traced here: 76 us
  Pallas kernels  68 us (89%)
  local copies, waits for them, and re-layouts  8.06 us (11%)
    pallas_call x1, Pallas kernels, body(): pl.pallas_call(functools.partial(section, fine, coarse, lats, lons), out_...  68 us
    unnamed x2, local copies, waits for them, and re-layouts  4.24 us

commit v1 on v0

--- a/solution.py
+++ b/solution.py
@@ -15,7 +15,8 @@
 HALF_LAT = WIN_LAT // 2
 HALF_LON = WIN_LON // 2
 HEAD = 32
-LANES = 128
+GROUP = 256
+LOG2E = math.log2(math.e)
 EPS = 1e-05
 EXCLUDED = -1e30
 MESH = pl.DeviceIdType.MESH
@@ -102,6 +103,10 @@
     return jnp.dot(a, b, preferred_element_type=F32)
 
 
+def across(a, b):
+    return lax.dot_general(a, b, (((1,), (1,)), ((), ())), preferred_element_type=F32)
+
+
 def pick(matrix, values):
     return dot(matrix, values).astype(BF16)
 
@@ -114,45 +119,69 @@
 
 
 def gelu(x):
-    return 0.5 * x * (1.0 + lax.erf(x * math.sqrt(0.5)))
-
-
-def attend(q_ref, k_ref, v_ref, out_ref, rows, bias_ref, mask):
-    size = mask.shape[0]
+    size = jnp.abs(x)
+    below = 1.0 + (0.3275911 * math.sqrt(0.5)) * size
+    t = pl.reciprocal(below, approx=True)
+    t = t * (2.0 - below * t)
+    tail = 0.5 * 1.061405429
+    for term in (-1.453152027, 1.421413741, -0.284496736, 0.254829592):
+        tail = tail * t + 0.5 * term
+    return jnp.maximum(x, 0.0) - (size * t) * (tail * jnp.exp2((x * x) * (-0.5 * LOG2E)))
+
+
+def attend(q_ref, k_ref, v_ref, out_ref, rows, bias_ref, fold_ref):
+    size = fold_ref.shape[0]
     width = q_ref.shape[-1]
-    for start in range(0, width, LANES):
-        lanes = slice(start, min(start + LANES, width))
+    for start in range(0, width, GROUP):
+        lanes = slice(start, min(start + GROUP, width))
         span = lanes.stop - start
         heads = span // HEAD
-        first = start // HEAD
+        spot = start // HEAD * size
         q = q_ref[rows, lanes]
-        lane = lax.broadcasted_iota(jnp.int32, (size, span), 1) // HEAD
-        stack = jnp.concatenate(
-            [jnp.where(lane == head, q, jnp.zeros_like(q)) for head in range(heads)], axis=0
+        lane = lax.broadcasted_iota(jnp.int32, (1, span), 1) // HEAD
+        stack = jnp.concatenate([q * (lane == head).astype(BF16) for head in range(heads)], axis=0)
+        scores = across(k_ref[rows, lanes], stack)
+        scores = scores * (LOG2E / math.sqrt(HEAD)) + bias_ref[:, spot : spot + heads * size]
+        raised = jnp.exp2(scores - jnp.max(scores, axis=0, keepdims=True))
+        factor = 1.0 / jnp.sum(raised, axis=0, keepdims=True)
+        mixed = lax.dot_general(
+            v_ref[rows, lanes], raised.astype(BF16), (((0,), (0,)), ((), ())), preferred_element_type=F32
         )
-        scores = lax.dot_general(
-            stack, k_ref[rows, lanes], (((1,), (1,)), ((), ())), preferred_element_type=F32
-        )
-        scores = scores * (1.0 / math.sqrt(HEAD)) + bias_ref[first * size : (first + heads) * size, :]
-        scores = (scores.reshape(heads, size, size) + mask[None]).reshape(heads * size, size)
-        highest = jnp.max(scores, axis=-1, keepdims=True)
-        raised = jnp.exp(scores - highest)
-        total = jnp.sum(raised, axis=-1, keepdims=True)
-        mixed = dot(raised.astype(BF16), v_ref[rows, lanes]) / total
-        result = jnp.zeros((size, span), F32)
-        for head in range(heads):
-            result = jnp.where(lane == head, mixed[head * size : (head + 1) * size], result)
-        out_ref[rows, lanes] = result.astype(BF16)
-
-
-def feed_forward(after, gain, up_ref, down_ref):
+        owner = lax.broadcasted_iota(jnp.int32, (1, heads * size), 1) // size
+        mixed = [
+            (mixed[head * HEAD : (head + 1) * HEAD] * jnp.where(owner == head, factor, 0.0)).astype(BF16)
+            for head in range(heads)
+        ]
+        mixed = jnp.concatenate(mixed, axis=0)
+        out_ref[rows, lanes] = across(fold_ref[:, : heads * size], mixed).astype(BF16)
+
+
+def score_tables(bias_ref, table_ref):
+    size = bias_ref.shape[1]
+    half = size // WIN_P
+    bias = jnp.transpose(bias_ref[...]) * LOG2E
+    key = lax.broadcasted_iota(jnp.int32, (size, 1), 0)
+    query = lax.rem(lax.broadcasted_iota(jnp.int32, (1, bias.shape[1]), 1), size)
+
+    def edge(token):
+        return lax.rem(token, half) // (HALF_LAT * WIN_LON)
+
+    by_level = jnp.where(key // half != query // half, EXCLUDED, 0.0)
+    by_row = jnp.where(edge(key) != edge(query), EXCLUDED, 0.0)
+    table_ref[0] = bias
+    table_ref[1] = bias + by_row
+    table_ref[2] = bias + by_level
+    table_ref[3] = bias + by_row + by_level
+
+
+def feed_forward(after, gain, up_ref, down):
     normed = layer_norm(after, gain).astype(BF16)
     total = after
     width = up_ref.shape[1]
     for start in range(0, width, 256):
         columns = slice(start, start + 256)
         hidden = gelu(dot(normed, up_ref[:, columns])).astype(BF16)
-        total = total + dot(hidden, down_ref[columns, :])
+        total = total + down(hidden, columns)
     return total.astype(BF16)
 
 
@@ -164,10 +193,10 @@
         up_first, up_norm, up_second,
         fine_send, fine_own, fine_halo, fine_send_back, fine_own_back, fine_halo_back, quarter, quarter_back,
         coarse_send, coarse_own, coarse_halo, coarse_send_back, coarse_own_back, coarse_halo_back,
-        level_mask, lat_mask,
+        fold,
         out,
         fine_normed, skip, coarse_in, coarse_normed, q_ref, k_ref, v_ref, attended, coarse_attended,
-        qc_ref, kc_ref, vc_ref, parts,
+        qc_ref, kc_ref, vc_ref, parts, fine_table, coarse_table,
         out_one, in_one, out_two, in_two, out_three, in_three, out_four, in_four,
         send_sems, recv_sems,
     ) = refs
@@ -211,10 +240,8 @@
     def field_pair(pair):
         return jnp.concatenate([field[2 * pair + 1], field[lax.rem(2 * pair + 2, depth)]], axis=0)
 
-    def level_flag(pair):
-        return jnp.where(pair == pairs - 1, 1.0, 0.0).astype(F32)
-
-    lat_flag = jnp.where(lat == lats - 1, 1.0, 0.0).astype(F32)
+    def table(pair, bottom):
+        return 2 * ((pair + 1) // pairs) + bottom * ((lat + 1) // lats)
 
     def send_fine(pair, carry):
         normed = layer_norm(field_pair(pair).astype(F32), a_norm_one[...]).astype(BF16)
@@ -229,6 +256,8 @@
     project = a_project[...]
     for part in range(3):
         parts[part] = project[:, part * width : (part + 1) * width]
+    score_tables(a_bias, fine_table)
+    score_tables(b_bias, coarse_table)
 
     def attend_fine(pair, carry):
         for copy in phase_one(pair):
@@ -236,14 +265,13 @@
         tokens = (dot(fine_own[...], fine_normed[pair]) + dot(fine_halo[...], in_one[pair])).astype(BF16)
         for part, ref in enumerate((q_ref, k_ref, v_ref)):
             ref[...] = dot(tokens, parts[part]).astype(BF16)
-        level = level_flag(pair) * level_mask[...]
-        across = fine.columns // WIN_LON
+        beside = fine.columns // WIN_LON
+        tall = fine.windows // beside
 
         def window(index, inner):
-            bottom = jnp.where(index >= fine.windows - across, lat_flag, 0.0)
-            mask = level + bottom * lat_mask[...]
             rows = pl.ds(pl.multiple_of(index * size, size), size)
-            attend(q_ref, k_ref, v_ref, attended.at[pair], rows, a_bias, mask)
+            scores = fine_table.at[table(pair, (index // beside + 1) // tall)]
+            attend(q_ref, k_ref, v_ref, attended.at[pair], rows, scores, fold)
             return inner
 
         lax.fori_loop(0, fine.windows, window, 0)
@@ -260,7 +288,9 @@
         mixed = (dot(fine_own_back[...], attended[pair]) + dot(fine_halo_back[...], in_two[pair])).astype(BF16)
         after = dot(quarter[...], field_pair(pair)) + dot(mixed, a_output[...])
         after = after.astype(BF16).astype(F32)
-        state = feed_forward(after, a_norm_two[...], a_raise, a_lower)
+        state = feed_forward(
+            after, a_norm_two[...], a_raise, lambda hidden, span: across(hidden, a_lower[:, span])
+        )
         skip[pair] = state
         quarters = [state[i * size : (i + 1) * size].astype(F32) for i in range(4)]
         average = sum(jnp.sum(values, axis=-1, keepdims=True) for values in quarters) / (4 * width)
@@ -268,8 +298,9 @@
         variance = sum(jnp.sum(values * values, axis=-1, keepdims=True) for values in centred) / (4 * width)
         factor = lax.rsqrt(variance + EPS)
         merged = jnp.zeros((size, merge_weight.shape[1]), F32)
+        gain = merge_gain[...].reshape(1, -1)
         for i in range(4):
-            normed = (centred[i] * factor * merge_gain[i]).astype(BF16)
+            normed = (centred[i] * factor * gain[:, i * width : (i + 1) * width]).astype(BF16)
             merged = merged + dot(normed, merge_weight[i * width : (i + 1) * width, :])
         merged = merged.astype(BF16)
         coarse_in[pair] = merged
@@ -289,8 +320,8 @@
         double = tokens.shape[1]
         for part, ref in enumerate((qc_ref, kc_ref, vc_ref)):
             ref[...] = dot(tokens, b_project[:, part * double : (part + 1) * double]).astype(BF16)
-        mask = level_flag(pair) * level_mask[...] + lat_flag * lat_mask[...]
-        attend(qc_ref, kc_ref, vc_ref, coarse_attended.at[pair], pl.ds(0, size), b_bias, mask)
+        scores = coarse_table.at[table(pair, 1)]
+        attend(qc_ref, kc_ref, vc_ref, coarse_attended.at[pair], pl.ds(0, size), scores, fold)
         out_four[pair] = pick(coarse_send_back[...], coarse_attended[pair])
         for copy in phase_four(pair):
             copy.start()
@@ -306,7 +337,9 @@
         ).astype(BF16)
         after = coarse_in[pair].astype(F32) + dot(mixed, b_output[...])
         after = after.astype(BF16).astype(F32)
-        state = feed_forward(after, b_norm_two[...], b_raise, b_lower)
+        state = feed_forward(
+            after, b_norm_two[...], b_raise, lambda hidden, span: dot(hidden, b_lower[span, :])
+        )
         raised = dot(state, up_first[...]).astype(BF16).astype(F32)
         raised = jnp.concatenate([raised[:, i * width : (i + 1) * width] for i in range(4)], axis=0)
         normed = layer_norm(raised, up_norm[...]).astype(BF16)
@@ -351,22 +384,17 @@
         quarter, quarter.T,
         coarse.send(), coarse_own, coarse_halo, coarse_halo.T, coarse_own.T, coarse.send().T,
     ]
-    token = np.arange(size)
-    level = token // (WIN_LAT * WIN_LON)
-    edge = (token // WIN_LON) % WIN_LAT >= WIN_LAT - HALF_LAT
-    masks = [
-        np.where(kind[:, None] != kind[None, :], EXCLUDED, 0.0).astype(np.float32) for kind in (level, edge)
-    ]
+    fold = np.tile(np.eye(size, dtype=np.float32), (1, GROUP // HEAD))
     operands = [
         field.reshape(depth, rows * columns, width),
-        a_norm_one.reshape(1, -1), a_project, a_bias.reshape(-1, size), a_output, a_norm_two.reshape(1, -1),
-        a_raise, a_lower,
-        merge_norm_gain.reshape(4, 1, width), merge_weight,
-        b_norm_one.reshape(1, -1), b_project, b_bias.reshape(-1, size), b_output, b_norm_two.reshape(1, -1),
+        a_norm_one, a_project, a_bias.reshape(-1, size), a_output, a_norm_two,
+        a_raise, a_lower.T,
+        merge_norm_gain, merge_weight,
+        b_norm_one, b_project, b_bias.reshape(-1, size), b_output, b_norm_two,
         b_raise, b_lower,
-        up_first, up_norm.reshape(1, -1), up_second,
+        up_first, up_norm, up_second,
     ]
-    operands += [one_hot(matrix) for matrix in orders] + [jnp.asarray(mask) for mask in masks]
+    operands += [one_hot(matrix) for matrix in orders + [fold]]
     vmem = pl.BlockSpec(memory_space=pltpu.VMEM)
     result = pl.pallas_call(
         functools.partial(section, fine, coarse, lats, lons),
@@ -387,6 +415,8 @@
             pltpu.VMEM((coarse.local, double), BF16),
             pltpu.VMEM((coarse.local, double), BF16),
             pltpu.VMEM((3, width, width), BF16),
+            pltpu.VMEM((4, size, a_bias.shape[0] * size), F32),
+            pltpu.VMEM((4, size, b_bias.shape[0] * size), F32),
         ]
         + [pltpu.VMEM((pairs, fine.halo, width), BF16)] * 4
         + [pltpu.VMEM((pairs, coarse.halo, double), BF16)] * 4

time: 76.3 us -> 75.7 us (level)
  local copies, waits for them, and re-layouts: 8.06 us -> 2.36 us
  Pallas kernels: 68 us -> 73.2 us
    pallas_call x1, Pallas kernels: 68 us -> 73.2 us  [body(): pl.pallas_call(functools.partial(section, fine, coarse, lats, lons), out_...]
    reshape x3 -> x0, local copies, waits for them, and re-layouts: 3.82 us -> none  [the longest x1 1.35 us: body(): merge_norm_gain.reshape(4, 1, width)]
    unnamed x2 -> x1, local copies, waits for them, and re-layouts: 4.24 us -> 2.36 us
where the time goes in v1:
time: 75.7 us; the launch traced here: 75.6 us
  Pallas kernels  73.2 us (97%)
  local copies, waits for them, and re-layouts  2.36 us (3%)
    pallas_call x1, Pallas kernels, body(): pl.pallas_call(functools.partial(section, fine, coarse, lats, lons), out_...  73.2 us
    unnamed x1, local copies, waits for them, and re-layouts  2.36 us

profile of v1, /device:TPU:0, one launch (start us, length us, event | category | flops | bytes accessed | tf_op | source)
XLA Modules:
  0.0 75.6 jit_solution(16263539406690526740)
XLA Ops:
  0.0 73.2 %shard_map.325 = bf16[8,288,192]{2,1,0:T(8,128)(2,1)} custom-call(bf16[8,288,192]{2,1,0:T(8,128)(2,1)} %bitcast.7, f32[192]{0:T(256)} %refs_1_.1, bf16[192,576]{1,0:T(8,128)(2,1)} %refs_2_.1, f32[864,144]{1,0:T(8,128)} %bitcast.8, bf16[192,192]{1,0:T(8,128)(2,1)} %refs_4_.1, f32[192]{0:T(256)} %refs_5_.1, bf16[192,768]{1,0:T(8,128)(2,1)} %refs_6_.1, ...), custom_call_target="tpu_custom_call" | custom-call | tf_op jit(solution)/shard_map/pallas_call | solution.py:399
  73.2 2.4 %copy.37 = bf16[8,12,24,192]{3,2,1,0:T(8,128)(2,1)} copy(bf16[8,12,24,192]{3,2,1,0:T(8,128)(2,1)} %bitcast.5) | data formatting | bytes 1769472

commit v2 on v1

--- a/solution.py
+++ b/solution.py
@@ -15,10 +15,11 @@
 HALF_LAT = WIN_LAT // 2
 HALF_LON = WIN_LON // 2
 HEAD = 32
-GROUP = 256
+GROUP = 128
 LOG2E = math.log2(math.e)
 EPS = 1e-05
 EXCLUDED = -1e30
+EARLY = 5
 MESH = pl.DeviceIdType.MESH
 BF16 = jnp.bfloat16
 F32 = jnp.float32
@@ -129,49 +130,29 @@
     return jnp.maximum(x, 0.0) - (size * t) * (tail * jnp.exp2((x * x) * (-0.5 * LOG2E)))
 
 
-def attend(q_ref, k_ref, v_ref, out_ref, rows, bias_ref, fold_ref):
-    size = fold_ref.shape[0]
-    width = q_ref.shape[-1]
+def attend(q_ref, k_ref, v_ref, out_ref, rows, bias_ref, query_code, key_code):
+    size = query_code.shape[0]
+    width = out_ref.shape[-1]
     for start in range(0, width, GROUP):
-        lanes = slice(start, min(start + GROUP, width))
-        span = lanes.stop - start
+        span = min(GROUP, width - start)
         heads = span // HEAD
-        spot = start // HEAD * size
+        first = start // HEAD
+        lanes = slice(start, start + GROUP)
         q = q_ref[rows, lanes]
-        lane = lax.broadcasted_iota(jnp.int32, (1, span), 1) // HEAD
+        lane = lax.broadcasted_iota(jnp.int32, (1, GROUP), 1) // HEAD
         stack = jnp.concatenate([q * (lane == head).astype(BF16) for head in range(heads)], axis=0)
-        scores = across(k_ref[rows, lanes], stack)
-        scores = scores * (LOG2E / math.sqrt(HEAD)) + bias_ref[:, spot : spot + heads * size]
-        raised = jnp.exp2(scores - jnp.max(scores, axis=0, keepdims=True))
-        factor = 1.0 / jnp.sum(raised, axis=0, keepdims=True)
-        mixed = lax.dot_general(
-            v_ref[rows, lanes], raised.astype(BF16), (((0,), (0,)), ((), ())), preferred_element_type=F32
-        )
-        owner = lax.broadcasted_iota(jnp.int32, (1, heads * size), 1) // size
-        mixed = [
-            (mixed[head * HEAD : (head + 1) * HEAD] * jnp.where(owner == head, factor, 0.0)).astype(BF16)
-            for head in range(heads)
-        ]
-        mixed = jnp.concatenate(mixed, axis=0)
-        out_ref[rows, lanes] = across(fold_ref[:, : heads * size], mixed).astype(BF16)
-
-
-def score_tables(bias_ref, table_ref):
-    size = bias_ref.shape[1]
-    half = size // WIN_P
-    bias = jnp.transpose(bias_ref[...]) * LOG2E
-    key = lax.broadcasted_iota(jnp.int32, (size, 1), 0)
-    query = lax.rem(lax.broadcasted_iota(jnp.int32, (1, bias.shape[1]), 1), size)
-
-    def edge(token):
-        return lax.rem(token, half) // (HALF_LAT * WIN_LON)
-
-    by_level = jnp.where(key // half != query // half, EXCLUDED, 0.0)
-    by_row = jnp.where(edge(key) != edge(query), EXCLUDED, 0.0)
-    table_ref[0] = bias
-    table_ref[1] = bias + by_row
-    table_ref[2] = bias + by_level
-    table_ref[3] = bias + by_row + by_level
+        stack = jnp.concatenate([stack, jnp.concatenate([query_code] * heads, axis=0)], axis=1)
+        scores = across(stack, jnp.concatenate([k_ref[rows, lanes], key_code], axis=1))
+        scores = scores + bias_ref[first * size : (first + heads) * size, :]
+        raised = jnp.exp2(scores - jnp.max(scores, axis=-1, keepdims=True)).astype(BF16)
+        mixed = dot(raised, v_ref[rows, 2 * start : 2 * start + 2 * GROUP])
+        total = mixed[:, GROUP:]
+        factor = pl.reciprocal(total, approx=True)
+        mixed = mixed[:, :GROUP] * (factor * (2.0 - total * factor))
+        result = mixed[:size]
+        for head in range(1, heads):
+            result = jnp.where(lane == head, mixed[head * size : (head + 1) * size], result)
+        out_ref[rows, start : start + span] = result[:, :span].astype(BF16)
 
 
 def feed_forward(after, gain, up_ref, down):
@@ -185,7 +166,22 @@
     return total.astype(BF16)
 
 
-def section(fine, coarse, lats, lons, *refs):
+def section(fine, coarse, lats, lons, places, *refs):
+    count = places[0]
+    moved = places[1:]
+    operands = list(refs[:count])
+    (
+        out,
+        fine_normed, skip, coarse_in, coarse_normed, q_ref, k_ref, v_ref, attended, coarse_attended,
+        qc_ref, kc_ref, vc_ref, parts, fine_table, coarse_table,
+        out_one, in_one, out_two, in_two, out_three, in_three, out_four, in_four,
+        send_sems, recv_sems, load_sems,
+    ) = refs[count : len(refs) - len(moved)]
+    loads = []
+    for slot, (place, held) in enumerate(zip(moved, refs[len(refs) - len(moved) :])):
+        loads.append(pltpu.make_async_copy(operands[place], held, load_sems.at[slot]))
+        loads[-1].start()
+        operands[place] = held
     (
         field, a_norm_one, a_project, a_bias, a_output, a_norm_two, a_raise, a_lower,
         merge_gain, merge_weight,
@@ -193,13 +189,8 @@
         up_first, up_norm, up_second,
         fine_send, fine_own, fine_halo, fine_send_back, fine_own_back, fine_halo_back, quarter, quarter_back,
         coarse_send, coarse_own, coarse_halo, coarse_send_back, coarse_own_back, coarse_halo_back,
-        fold,
-        out,
-        fine_normed, skip, coarse_in, coarse_normed, q_ref, k_ref, v_ref, attended, coarse_attended,
-        qc_ref, kc_ref, vc_ref, parts, fine_table, coarse_table,
-        out_one, in_one, out_two, in_two, out_three, in_three, out_four, in_four,
-        send_sems, recv_sems,
-    ) = refs
+        query_code, level_code, edge_code,
+    ) = operands
     depth = field.shape[0]
     pairs = depth // WIN_P
     width = field.shape[2]
@@ -240,8 +231,20 @@
     def field_pair(pair):
         return jnp.concatenate([field[2 * pair + 1], field[lax.rem(2 * pair + 2, depth)]], axis=0)
 
-    def table(pair, bottom):
-        return 2 * ((pair + 1) // pairs) + bottom * ((lat + 1) // lats)
+    def key_code(pair, bottom):
+        level = ((pair + 1) // pairs).astype(F32)
+        edge = (bottom * ((lat + 1) // lats)).astype(F32)
+        return (level * level_code[...] + edge * edge_code[...]).astype(BF16)
+
+    def project(tokens, weights, out_refs):
+        q_out, k_out, v_out = out_refs
+        q_out[...] = (dot(tokens, weights(0)) * (LOG2E / math.sqrt(HEAD))).astype(BF16)
+        k_out[...] = dot(tokens, weights(1)).astype(BF16)
+        values = dot(tokens, weights(2)).astype(BF16)
+        ones = jnp.ones((values.shape[0], GROUP), BF16)
+        for start in range(0, values.shape[1], GROUP):
+            v_out[:, 2 * start : 2 * start + GROUP] = values[:, start : start + GROUP]
+            v_out[:, 2 * start + GROUP : 2 * start + 2 * GROUP] = ones
 
     def send_fine(pair, carry):
         normed = layer_norm(field_pair(pair).astype(F32), a_norm_one[...]).astype(BF16)
@@ -253,34 +256,36 @@
 
     lax.fori_loop(0, pairs, send_fine, 0)
 
-    project = a_project[...]
+    for load in loads[:EARLY]:
+        load.wait()
+    parts[...] = jnp.zeros_like(parts)
+    joined = a_project[...]
     for part in range(3):
-        parts[part] = project[:, part * width : (part + 1) * width]
-    score_tables(a_bias, fine_table)
-    score_tables(b_bias, coarse_table)
+        parts[part, :, :width] = joined[:, part * width : (part + 1) * width]
+    fine_table[...] = a_bias[...] * LOG2E
 
     def attend_fine(pair, carry):
         for copy in phase_one(pair):
             copy.wait_recv()
         tokens = (dot(fine_own[...], fine_normed[pair]) + dot(fine_halo[...], in_one[pair])).astype(BF16)
-        for part, ref in enumerate((q_ref, k_ref, v_ref)):
-            ref[...] = dot(tokens, parts[part]).astype(BF16)
+        project(tokens, lambda part: parts[part], (q_ref, k_ref, v_ref))
         beside = fine.columns // WIN_LON
         tall = fine.windows // beside
 
-        def window(index, inner):
-            rows = pl.ds(pl.multiple_of(index * size, size), size)
-            scores = fine_table.at[table(pair, (index // beside + 1) // tall)]
-            attend(q_ref, k_ref, v_ref, attended.at[pair], rows, scores, fold)
-            return inner
-
-        lax.fori_loop(0, fine.windows, window, 0)
+        for index in range(fine.windows):
+            code = key_code(pair, (index // beside + 1) // tall)
+            rows = slice(index * size, (index + 1) * size)
+            attend(q_ref, k_ref, v_ref, attended.at[pair], rows, fine_table, query_code[...], code)
         out_two[pair] = pick(fine_send_back[...], attended[pair])
         for copy in phase_two(pair):
             copy.start()
         return carry
 
     lax.fori_loop(0, pairs, attend_fine, 0)
+
+    for load in loads[EARLY:]:
+        load.wait()
+    coarse_table[...] = b_bias[...] * LOG2E
 
     def finish_fine(pair, carry):
         for copy in phase_two(pair):
@@ -318,10 +323,12 @@
             copy.wait_recv()
         tokens = (dot(coarse_own[...], coarse_normed[pair]) + dot(coarse_halo[...], in_three[pair])).astype(BF16)
         double = tokens.shape[1]
-        for part, ref in enumerate((qc_ref, kc_ref, vc_ref)):
-            ref[...] = dot(tokens, b_project[:, part * double : (part + 1) * double]).astype(BF16)
-        scores = coarse_table.at[table(pair, 1)]
-        attend(qc_ref, kc_ref, vc_ref, coarse_attended.at[pair], pl.ds(0, size), scores, fold)
+        weights = lambda part: b_project[:, part * double : (part + 1) * double]
+        project(tokens, weights, (qc_ref, kc_ref, vc_ref))
+        attend(
+            qc_ref, kc_ref, vc_ref, coarse_attended.at[pair], slice(0, size), coarse_table, query_code[...],
+            key_code(pair, 1),
+        )
         out_four[pair] = pick(coarse_send_back[...], coarse_attended[pair])
         for copy in phase_four(pair):
             copy.start()
@@ -384,7 +391,15 @@
         quarter, quarter.T,
         coarse.send(), coarse_own, coarse_halo, coarse_halo.T, coarse_own.T, coarse.send().T,
     ]
-    fold = np.tile(np.eye(size, dtype=np.float32), (1, GROUP // HEAD))
+    token = np.arange(size)
+    level = token // (WIN_LAT * WIN_LON)
+    edge = (token // WIN_LON) % WIN_LAT // HALF_LAT
+    codes = np.zeros((3, size, GROUP), np.float32)
+    for kind, flags in enumerate((level, edge)):
+        codes[0, :, 2 * kind], codes[0, :, 2 * kind + 1] = flags, 1 - flags
+        codes[kind + 1, :, 2 * kind], codes[kind + 1, :, 2 * kind + 1] = (
+            EXCLUDED * (1 - flags), EXCLUDED * flags
+        )
     operands = [
         field.reshape(depth, rows * columns, width),
         a_norm_one, a_project, a_bias.reshape(-1, size), a_output, a_norm_two,
@@ -394,33 +409,40 @@
         b_raise, b_lower,
         up_first, up_norm, up_second,
     ]
-    operands += [one_hot(matrix) for matrix in orders + [fold]]
+    operands += [one_hot(matrix) for matrix in orders + [codes[0]]] + [jnp.asarray(code) for code in codes[1:]]
     vmem = pl.BlockSpec(memory_space=pltpu.VMEM)
+    specs = [vmem] * len(operands)
+    moved = [2, 3, 21, 22, 23, 24, 25, 26, 4, 6, 7, 9, 28, 29, 30, 11, 12, 31, 32, 33, 13, 15, 16, 17, 19, 27]
+    for place in moved:
+        specs[place] = pl.BlockSpec(memory_space=pl.ANY)
+    wide = pl.cdiv(width, GROUP) * GROUP
     result = pl.pallas_call(
-        functools.partial(section, fine, coarse, lats, lons),
+        functools.partial(section, fine, coarse, lats, lons, [len(operands)] + moved),
         out_shape=jax.ShapeDtypeStruct((depth, rows * columns, width), BF16),
-        in_specs=[vmem] * len(operands),
+        in_specs=specs,
         out_specs=vmem,
         scratch_shapes=[
             pltpu.VMEM((pairs, fine.local, width), BF16),
             pltpu.VMEM((pairs, fine.local, width), BF16),
             pltpu.VMEM((pairs, coarse.local, double), BF16),
             pltpu.VMEM((pairs, coarse.local, double), BF16),
-            pltpu.VMEM((fine.local, width), BF16),
-            pltpu.VMEM((fine.local, width), BF16),
-            pltpu.VMEM((fine.local, width), BF16),
+            pltpu.VMEM((fine.local, wide), BF16),
+            pltpu.VMEM((fine.local, wide), BF16),
+            pltpu.VMEM((fine.local, 2 * wide), BF16),
             pltpu.VMEM((pairs, fine.local, width), BF16),
             pltpu.VMEM((pairs, coarse.local, double), BF16),
             pltpu.VMEM((coarse.local, double), BF16),
             pltpu.VMEM((coarse.local, double), BF16),
-            pltpu.VMEM((coarse.local, double), BF16),
-            pltpu.VMEM((3, width, width), BF16),
-            pltpu.VMEM((4, size, a_bias.shape[0] * size), F32),
-            pltpu.VMEM((4, size, b_bias.shape[0] * size), F32),
+            pltpu.VMEM((coarse.local, 2 * double), BF16),
+            pltpu.VMEM((3, width, wide), BF16),
+            pltpu.VMEM((a_bias.shape[0] * size, size), F32),
+            pltpu.VMEM((b_bias.shape[0] * size, size), F32),
         ]
         + [pltpu.VMEM((pairs, fine.halo, width), BF16)] * 4
         + [pltpu.VMEM((pairs, coarse.halo, double), BF16)] * 4
-        + [pltpu.SemaphoreType.DMA((4, pairs, 3)), pltpu.SemaphoreType.DMA((4, pairs, 3))],
+        + [pltpu.SemaphoreType.DMA((4, pairs, 3)), pltpu.SemaphoreType.DMA((4, pairs, 3))]
+        + [pltpu.SemaphoreType.DMA((len(moved),))]
+        + [pltpu.VMEM(operands[place].shape, operands[place].dtype) for place in moved],
         compiler_params=pltpu.CompilerParams(
             collective_id=0, has_side_effects=True, vmem_limit_bytes=56 * 1024 * 1024
         ),

time: 75.7 us -> 65.7 us (0.87)
  Pallas kernels: 73.2 us -> 63.1 us
    pallas_call x1, Pallas kernels: 73.2 us -> 63.1 us  [body(): pl.pallas_call(functools.partial(section, fine, coarse, lats, lons, [len(...]
where the time goes in v2:
time: 65.7 us; the launch traced here: 65.5 us
  Pallas kernels  63.1 us (96%)
  local copies, waits for them, and re-layouts  2.36 us (4%)
    pallas_call x1, Pallas kernels, body(): pl.pallas_call(functools.partial(section, fine, coarse, lats, lons, [len(...  63.1 us
    unnamed x1, local copies, waits for them, and re-layouts  2.36 us

profile of v2, /device:TPU:0, one launch (start us, length us, event | category | flops | bytes accessed | tf_op | source)
XLA Modules:
  0.0 65.5 jit_solution(4438235787277317803)
XLA Ops:
  0.0 63.1 %shard_map.343 = bf16[8,288,192]{2,1,0:T(8,128)(2,1)} custom-call(bf16[8,288,192]{2,1,0:T(8,128)(2,1)} %bitcast.7, f32[192]{0:T(256)} %refs_1_.1, bf16[192,576]{1,0:T(8,128)(2,1)} %refs_2_.1, f32[864,144]{1,0:T(8,128)} %bitcast.8, bf16[192,192]{1,0:T(8,128)(2,1)} %refs_4_.1, f32[192]{0:T(256)} %refs_5_.1, bf16[192,768]{1,0:T(8,128)(2,1)} %refs_6_.1, ...), custom_call_target="tpu_custom_call" | custom-call | tf_op jit(solution)/shard_map/pallas_call | solution.py:419
  63.1 2.4 %copy.39 = bf16[8,12,24,192]{3,2,1,0:T(8,128)(2,1)} copy(bf16[8,12,24,192]{3,2,1,0:T(8,128)(2,1)} %bitcast.5) | data formatting | bytes 1769472

commit v3 on v2

--- a/solution.py
+++ b/solution.py
@@ -20,6 +20,7 @@
 EPS = 1e-05
 EXCLUDED = -1e30
 EARLY = 5
+TOGETHER = 2
 MESH = pl.DeviceIdType.MESH
 BF16 = jnp.bfloat16
 F32 = jnp.float32
@@ -173,7 +174,7 @@
     (
         out,
         fine_normed, skip, coarse_in, coarse_normed, q_ref, k_ref, v_ref, attended, coarse_attended,
-        qc_ref, kc_ref, vc_ref, parts, fine_table, coarse_table,
+        qc_ref, kc_ref, vc_ref, coarse_both, parts, fine_table, coarse_table,
         out_one, in_one, out_two, in_two, out_three, in_three, out_four, in_four,
         send_sems, recv_sems, load_sems,
     ) = refs[count : len(refs) - len(moved)]
@@ -287,76 +288,109 @@
         load.wait()
     coarse_table[...] = b_bias[...] * LOG2E
 
-    def finish_fine(pair, carry):
-        for copy in phase_two(pair):
-            copy.wait_recv()
-        mixed = (dot(fine_own_back[...], attended[pair]) + dot(fine_halo_back[...], in_two[pair])).astype(BF16)
-        after = dot(quarter[...], field_pair(pair)) + dot(mixed, a_output[...])
-        after = after.astype(BF16).astype(F32)
-        state = feed_forward(
-            after, a_norm_two[...], a_raise, lambda hidden, span: across(hidden, a_lower[:, span])
-        )
-        skip[pair] = state
-        quarters = [state[i * size : (i + 1) * size].astype(F32) for i in range(4)]
+    def chosen(step):
+        return [TOGETHER * step + each for each in range(TOGETHER)]
+
+    def split(values):
+        return [values[each * size : (each + 1) * size] for each in range(TOGETHER)]
+
+    def join(values):
+        return jnp.concatenate(values, axis=0)
+
+    def finish_fine(step, carry):
+        for pair in chosen(step):
+            for copy in phase_two(pair):
+                copy.wait_recv()
+        states = []
+        for pair in chosen(step):
+            mixed = dot(fine_own_back[...], attended[pair]) + dot(fine_halo_back[...], in_two[pair])
+            after = dot(quarter[...], field_pair(pair)) + dot(mixed.astype(BF16), a_output[...])
+            after = after.astype(BF16).astype(F32)
+            states.append(
+                feed_forward(after, a_norm_two[...], a_raise, lambda hidden, span: across(hidden, a_lower[:, span]))
+            )
+            skip[pair] = states[-1]
+        quarters = [
+            join([state[i * size : (i + 1) * size] for state in states]).astype(F32) for i in range(4)
+        ]
         average = sum(jnp.sum(values, axis=-1, keepdims=True) for values in quarters) / (4 * width)
         centred = [values - average for values in quarters]
         variance = sum(jnp.sum(values * values, axis=-1, keepdims=True) for values in centred) / (4 * width)
         factor = lax.rsqrt(variance + EPS)
-        merged = jnp.zeros((size, merge_weight.shape[1]), F32)
+        merged = jnp.zeros((TOGETHER * size, merge_weight.shape[1]), F32)
         gain = merge_gain[...].reshape(1, -1)
         for i in range(4):
             normed = (centred[i] * factor * gain[:, i * width : (i + 1) * width]).astype(BF16)
             merged = merged + dot(normed, merge_weight[i * width : (i + 1) * width, :])
         merged = merged.astype(BF16)
-        coarse_in[pair] = merged
         normed = layer_norm(merged.astype(F32), b_norm_one[...]).astype(BF16)
-        coarse_normed[pair] = normed
-        out_three[pair] = pick(coarse_send[...], normed)
-        for copy in phase_three(pair):
-            copy.start()
-        return carry
-
-    lax.fori_loop(0, pairs, finish_fine, 0)
-
-    def attend_coarse(pair, carry):
-        for copy in phase_three(pair):
-            copy.wait_recv()
-        tokens = (dot(coarse_own[...], coarse_normed[pair]) + dot(coarse_halo[...], in_three[pair])).astype(BF16)
+        for pair, plain, ready in zip(chosen(step), split(merged), split(normed)):
+            out_three[pair] = pick(coarse_send[...], ready)
+            for copy in phase_three(pair):
+                copy.start()
+            coarse_in[pair] = plain
+            coarse_normed[pair] = ready
+        return carry
+
+    lax.fori_loop(0, pairs // TOGETHER, finish_fine, 0)
+
+    def attend_coarse(step, carry):
+        for pair in chosen(step):
+            for copy in phase_three(pair):
+                copy.wait_recv()
+        tokens = join(
+            [
+                dot(coarse_own[...], coarse_normed[pair]) + dot(coarse_halo[...], in_three[pair])
+                for pair in chosen(step)
+            ]
+        ).astype(BF16)
         double = tokens.shape[1]
         weights = lambda part: b_project[:, part * double : (part + 1) * double]
         project(tokens, weights, (qc_ref, kc_ref, vc_ref))
-        attend(
-            qc_ref, kc_ref, vc_ref, coarse_attended.at[pair], slice(0, size), coarse_table, query_code[...],
-            key_code(pair, 1),
-        )
-        out_four[pair] = pick(coarse_send_back[...], coarse_attended[pair])
-        for copy in phase_four(pair):
-            copy.start()
-        return carry
-
-    lax.fori_loop(0, pairs, attend_coarse, 0)
-
-    def finish_coarse(pair, carry):
-        for copy in phase_four(pair):
-            copy.wait_recv()
-        mixed = (
-            dot(coarse_own_back[...], coarse_attended[pair]) + dot(coarse_halo_back[...], in_four[pair])
+        for each, pair in enumerate(chosen(step)):
+            attend(
+                qc_ref, kc_ref, vc_ref, coarse_both, slice(each * size, (each + 1) * size), coarse_table,
+                query_code[...], key_code(pair, 1),
+            )
+        for each, pair in enumerate(chosen(step)):
+            mixed = coarse_both[each * size : (each + 1) * size]
+            out_four[pair] = pick(coarse_send_back[...], mixed)
+            for copy in phase_four(pair):
+                copy.start()
+            coarse_attended[pair] = mixed
+        return carry
+
+    lax.fori_loop(0, pairs // TOGETHER, attend_coarse, 0)
+
+    def finish_coarse(step, carry):
+        for pair in chosen(step):
+            for copy in phase_four(pair):
+                copy.wait_recv()
+        mixed = join(
+            [
+                dot(coarse_own_back[...], coarse_attended[pair]) + dot(coarse_halo_back[...], in_four[pair])
+                for pair in chosen(step)
+            ]
         ).astype(BF16)
-        after = coarse_in[pair].astype(F32) + dot(mixed, b_output[...])
+        after = join([coarse_in[pair] for pair in chosen(step)]).astype(F32) + dot(mixed, b_output[...])
         after = after.astype(BF16).astype(F32)
         state = feed_forward(
             after, b_norm_two[...], b_raise, lambda hidden, span: dot(hidden, b_lower[span, :])
         )
         raised = dot(state, up_first[...]).astype(BF16).astype(F32)
-        raised = jnp.concatenate([raised[:, i * width : (i + 1) * width] for i in range(4)], axis=0)
+        raised = join([raised[:, i * width : (i + 1) * width] for i in range(4)])
         normed = layer_norm(raised, up_norm[...]).astype(BF16)
-        total = (skip[pair].astype(F32) + dot(normed, up_second[...])).astype(BF16)
-        total = pick(quarter_back[...], total)
-        out[2 * pair + 1] = total[:level_size]
-        out[lax.rem(2 * pair + 2, depth)] = total[level_size:]
-        return carry
-
-    lax.fori_loop(0, pairs, finish_coarse, 0)
+        added = dot(normed, up_second[...])
+        for each, pair in enumerate(chosen(step)):
+            own = join(
+                [added[(i * TOGETHER + each) * size : (i * TOGETHER + each + 1) * size] for i in range(4)]
+            )
+            total = pick(quarter_back[...], (skip[pair].astype(F32) + own).astype(BF16))
+            out[2 * pair + 1] = total[:level_size]
+            out[lax.rem(2 * pair + 2, depth)] = total[level_size:]
+        return carry
+
+    lax.fori_loop(0, pairs // TOGETHER, finish_coarse, 0)
 
     def drain(pair, carry):
         for phase in (phase_one, phase_two, phase_three, phase_four):
@@ -431,9 +465,10 @@
             pltpu.VMEM((fine.local, 2 * wide), BF16),
             pltpu.VMEM((pairs, fine.local, width), BF16),
             pltpu.VMEM((pairs, coarse.local, double), BF16),
-            pltpu.VMEM((coarse.local, double), BF16),
-            pltpu.VMEM((coarse.local, double), BF16),
-            pltpu.VMEM((coarse.local, 2 * double), BF16),
+            pltpu.VMEM((TOGETHER * coarse.local, double), BF16),
+            pltpu.VMEM((TOGETHER * coarse.local, double), BF16),
+            pltpu.VMEM((TOGETHER * coarse.local, 2 * double), BF16),
+            pltpu.VMEM((TOGETHER * coarse.local, double), BF16),
             pltpu.VMEM((3, width, wide), BF16),
             pltpu.VMEM((a_bias.shape[0] * size, size), F32),
             pltpu.VMEM((b_bias.shape[0] * size, size), F32),

time: 65.7 us -> 61.5 us (0.936)
  Pallas kernels: 63.1 us -> 58.9 us
    pallas_call x1, Pallas kernels: 63.1 us -> 58.9 us  [body(): pl.pallas_call(functools.partial(section, fine, coarse, lats, lons, [len(...]
where the time goes in v3:
time: 61.5 us; the launch traced here: 61.3 us
  Pallas kernels  58.9 us (96%)
  local copies, waits for them, and re-layouts  2.36 us (4%)
    pallas_call x1, Pallas kernels, body(): pl.pallas_call(functools.partial(section, fine, coarse, lats, lons, [len(...  58.9 us
    unnamed x1, local copies, waits for them, and re-layouts  2.36 us

profile of v3, /device:TPU:0, one launch (start us, length us, event | category | flops | bytes accessed | tf_op | source)
XLA Modules:
  0.0 61.3 jit_solution(1041299427789656319)
XLA Ops:
  0.0 58.9 %shard_map.343 = bf16[8,288,192]{2,1,0:T(8,128)(2,1)} custom-call(bf16[8,288,192]{2,1,0:T(8,128)(2,1)} %bitcast.7, f32[192]{0:T(256)} %refs_1_.1, bf16[192,576]{1,0:T(8,128)(2,1)} %refs_2_.1, f32[864,144]{1,0:T(8,128)} %bitcast.8, bf16[192,192]{1,0:T(8,128)(2,1)} %refs_4_.1, f32[192]{0:T(256)} %refs_5_.1, bf16[192,768]{1,0:T(8,128)(2,1)} %refs_6_.1, ...), custom_call_target="tpu_custom_call" | custom-call | tf_op jit(solution)/shard_map/pallas_call | solution.py:453
  58.9 2.4 %copy.39 = bf16[8,12,24,192]{3,2,1,0:T(8,128)(2,1)} copy(bf16[8,12,24,192]{3,2,1,0:T(8,128)(2,1)} %bitcast.5) | data formatting | bytes 1769472

commit v4 on v3

--- a/solution.py
+++ b/solution.py
@@ -121,14 +121,17 @@
 
 
 def gelu(x):
+    x = x.astype(BF16)
+
+    def number(value):
+        return jnp.asarray(value, BF16)
+
     size = jnp.abs(x)
-    below = 1.0 + (0.3275911 * math.sqrt(0.5)) * size
-    t = pl.reciprocal(below, approx=True)
-    t = t * (2.0 - below * t)
-    tail = 0.5 * 1.061405429
+    t = pl.reciprocal(number(1.0) + number(0.3275911 * math.sqrt(0.5)) * size, approx=True)
+    tail = number(0.5 * 1.061405429)
     for term in (-1.453152027, 1.421413741, -0.284496736, 0.254829592):
-        tail = tail * t + 0.5 * term
-    return jnp.maximum(x, 0.0) - (size * t) * (tail * jnp.exp2((x * x) * (-0.5 * LOG2E)))
+        tail = tail * t + number(0.5 * term)
+    return jnp.maximum(x, number(0.0)) - (size * t) * (tail * jnp.exp2((x * x) * number(-0.5 * LOG2E)))
 
 
 def attend(q_ref, k_ref, v_ref, out_ref, rows, bias_ref, query_code, key_code):
@@ -162,7 +165,7 @@
     width = up_ref.shape[1]
     for start in range(0, width, 256):
         columns = slice(start, start + 256)
-        hidden = gelu(dot(normed, up_ref[:, columns])).astype(BF16)
+        hidden = gelu(dot(normed, up_ref[:, columns]))
         total = total + down(hidden, columns)
     return total.astype(BF16)
 
@@ -174,7 +177,7 @@
     (
         out,
         fine_normed, skip, coarse_in, coarse_normed, q_ref, k_ref, v_ref, attended, coarse_attended,
-        qc_ref, kc_ref, vc_ref, coarse_both, parts, fine_table, coarse_table,
+        qc_ref, kc_ref, vc_ref, coarse_both, fine_both, parts, fine_table, coarse_table,
         out_one, in_one, out_two, in_two, out_three, in_three, out_four, in_four,
         send_sems, recv_sems, load_sems,
     ) = refs[count : len(refs) - len(moved)]
@@ -265,31 +268,36 @@
         parts[part, :, :width] = joined[:, part * width : (part + 1) * width]
     fine_table[...] = a_bias[...] * LOG2E
 
-    def attend_fine(pair, carry):
-        for copy in phase_one(pair):
-            copy.wait_recv()
-        tokens = (dot(fine_own[...], fine_normed[pair]) + dot(fine_halo[...], in_one[pair])).astype(BF16)
-        project(tokens, lambda part: parts[part], (q_ref, k_ref, v_ref))
+    def chosen(step):
+        return [TOGETHER * step + each for each in range(TOGETHER)]
+
+    def attend_fine(step, carry):
+        for pair in chosen(step):
+            for copy in phase_one(pair):
+                copy.wait_recv()
         beside = fine.columns // WIN_LON
         tall = fine.windows // beside
-
-        for index in range(fine.windows):
-            code = key_code(pair, (index // beside + 1) // tall)
-            rows = slice(index * size, (index + 1) * size)
-            attend(q_ref, k_ref, v_ref, attended.at[pair], rows, fine_table, query_code[...], code)
-        out_two[pair] = pick(fine_send_back[...], attended[pair])
-        for copy in phase_two(pair):
-            copy.start()
+        for each, pair in enumerate(chosen(step)):
+            tokens = (dot(fine_own[...], fine_normed[pair]) + dot(fine_halo[...], in_one[pair])).astype(BF16)
+            held = (q_ref.at[each], k_ref.at[each], v_ref.at[each])
+            project(tokens, lambda part: parts[part], held)
+            for index in range(fine.windows):
+                code = key_code(pair, (index // beside + 1) // tall)
+                rows = slice(index * size, (index + 1) * size)
+                attend(*held, fine_both.at[each], rows, fine_table, query_code[...], code)
+        for each, pair in enumerate(chosen(step)):
+            mixed = fine_both[each]
+            out_two[pair] = pick(fine_send_back[...], mixed)
+            for copy in phase_two(pair):
+                copy.start()
+            attended[pair] = mixed
         return carry
 
-    lax.fori_loop(0, pairs, attend_fine, 0)
+    lax.fori_loop(0, pairs // TOGETHER, attend_fine, 0)
 
     for load in loads[EARLY:]:
         load.wait()
     coarse_table[...] = b_bias[...] * LOG2E
-
-    def chosen(step):
-        return [TOGETHER * step + each for each in range(TOGETHER)]
 
     def split(values):
         return [values[each * size : (each + 1) * size] for each in range(TOGETHER)]
@@ -460,15 +468,16 @@
             pltpu.VMEM((pairs, fine.local, width), BF16),
             pltpu.VMEM((pairs, coarse.local, double), BF16),
             pltpu.VMEM((pairs, coarse.local, double), BF16),
-            pltpu.VMEM((fine.local, wide), BF16),
-            pltpu.VMEM((fine.local, wide), BF16),
-            pltpu.VMEM((fine.local, 2 * wide), BF16),
+            pltpu.VMEM((TOGETHER, fine.local, wide), BF16),
+            pltpu.VMEM((TOGETHER, fine.local, wide), BF16),
+            pltpu.VMEM((TOGETHER, fine.local, 2 * wide), BF16),
             pltpu.VMEM((pairs, fine.local, width), BF16),
             pltpu.VMEM((pairs, coarse.local, double), BF16),
             pltpu.VMEM((TOGETHER * coarse.local, double), BF16),
             pltpu.VMEM((TOGETHER * coarse.local, double), BF16),
             pltpu.VMEM((TOGETHER * coarse.local, 2 * double), BF16),
             pltpu.VMEM((TOGETHER * coarse.local, double), BF16),
+            pltpu.VMEM((TOGETHER, fine.local, width), BF16),
             pltpu.VMEM((3, width, wide), BF16),
             pltpu.VMEM((a_bias.shape[0] * size, size), F32),
             pltpu.VMEM((b_bias.shape[0] * size, size), F32),

time: 61.5 us -> 58.9 us (0.958)
  Pallas kernels: 58.9 us -> 56.4 us
    pallas_call x1, Pallas kernels: 58.9 us -> 56.4 us  [body(): pl.pallas_call(functools.partial(section, fine, coarse, lats, lons, [len(...]
where the time goes in v4:
time: 58.9 us; the launch traced here: 58.7 us
  Pallas kernels  56.4 us (96%)
  local copies, waits for them, and re-layouts  2.36 us (4%)
    pallas_call x1, Pallas kernels, body(): pl.pallas_call(functools.partial(section, fine, coarse, lats, lons, [len(...  56.4 us
    unnamed x1, local copies, waits for them, and re-layouts  2.36 us

profile of v4, /device:TPU:0, one launch (start us, length us, event | category | flops | bytes accessed | tf_op | source)
XLA Modules:
  0.0 58.7 jit_solution(14192694070416371378)
XLA Ops:
  0.0 56.4 %shard_map.343 = bf16[8,288,192]{2,1,0:T(8,128)(2,1)} custom-call(bf16[8,288,192]{2,1,0:T(8,128)(2,1)} %bitcast.7, f32[192]{0:T(256)} %refs_1_.1, bf16[192,576]{1,0:T(8,128)(2,1)} %refs_2_.1, f32[864,144]{1,0:T(8,128)} %bitcast.8, bf16[192,192]{1,0:T(8,128)(2,1)} %refs_4_.1, f32[192]{0:T(256)} %refs_5_.1, bf16[192,768]{1,0:T(8,128)(2,1)} %refs_6_.1, ...), custom_call_target="tpu_custom_call" | custom-call | tf_op jit(solution)/shard_map/pallas_call | solution.py:461
  56.4 2.4 %copy.39 = bf16[8,12,24,192]{3,2,1,0:T(8,128)(2,1)} copy(bf16[8,12,24,192]{3,2,1,0:T(8,128)(2,1)} %bitcast.5) | data formatting | bytes 1769472
